TPU v7x, 32 devices: a whole 2x2x4 slice. The times are simulated.
32 devices in a mesh: gx: 8 (over y, x, core), gy: 4 (over z).
Axes of the slice: x: 2, y: 2, z: 4, core: 2. Of those that a mesh axis runs over, the one named last changes fastest.
Arguments:
- fields: float32 [3, 8, 768, 512], P(None, None, 'gx', 'gy'), may hold values from -6 to 6
- terrain: int32 [768, 512], P('gx', 'gy'), may hold values from 0 to 2999
- parent_columns: bfloat16 [3, 60, 12288], P(None, None, ('gx', 'gy')), may hold values from -6 to 6
- record_tile: int32 [12288, 1], P(('gx', 'gy')), may hold values from 0 to 7; in each aligned block of 384 rows (0 to 383, 384 to 767, ...) at most 96 rows name the same one
- record_cells: int32 [12288, 4], P(('gx', 'gy')), may hold values from 0 to 191
- record_weights: bfloat16 [12288, 4], P(('gx', 'gy')), may hold values from 0.049804688 to 1
Outputs:
- updated_state: float32 [3, 8, 768, 512], P(None, None, 'gx', 'gy')
- nudge_coeffs: float32 [3, 8, 32, 32], replicated
Inputs may be any that keep to these rules, and one draw needn't show every extreme that they name: `record_tile`: at most 96 of the 384 records of one device name the same tile index, and some device names one tile index exactly 96 times.
All inputs are finite; a program needn't handle non-finite values.
Results may differ from a plain program's by a relative error of at most 0.0003.
Values may be sent and summed in bfloat16 or wider, within the bound.
A program may use at most 64 MiB of HBM per device.

v0:
```python
import functools
import math

import jax
import jax.numpy as jnp
import ml_dtypes
import numpy as np
from jax import lax
from jax.experimental import pallas as pl
from jax.experimental.pallas import tpu as pltpu
from jax.sharding import PartitionSpec as P

KW = 32
RATIO = 8
TOP = 12000.0
MESH = pl.DeviceIdType.MESH
F32 = jnp.float32
BF16 = jnp.bfloat16
NT = (((1,), (1,)), ((), ()))


def wave_rows(length):
    half = KW // 2
    x = np.arange(length, dtype=np.int64)
    rows = [np.ones(length)]
    for m in range(1, KW):
        if m < half:
            rows.append(math.sqrt(2.0) * np.cos(2.0 * math.pi * ((m * x) % length) / length))
        else:
            rows.append(
                math.sqrt(2.0) * np.sin(2.0 * math.pi * (((m - half + 1) * x) % length) / length)
            )
    return np.stack(rows)


def parts(values):
    values = values.astype(np.float32)
    high = values.astype(ml_dtypes.bfloat16)
    low = (values - high.astype(np.float32)).astype(ml_dtypes.bfloat16)
    return high, low


@functools.lru_cache(maxsize=None)
def tables(n_x, n_y, cells_x, cells_y, fields_count):
    total_x, total_y = n_x * cells_x, n_y * cells_y
    scale = 1.0 / math.sqrt(total_x * total_y)
    basis_x, basis_y = wave_rows(total_x), wave_rows(total_y)
    coarse_y = cells_y // RATIO
    own_x = np.transpose(basis_x.reshape(KW, n_x, cells_x), (1, 0, 2))
    high, low = parts(own_x * scale)
    project_x = np.concatenate(
        [np.concatenate([high, high], 2), np.concatenate([low, np.zeros_like(low)], 2)], 1
    )
    high, low = parts(np.transpose(own_x, (0, 2, 1)) * (4.0 * scale))
    expand_x = np.concatenate([high, low, high], 2)
    at_coarse = basis_x[:, ::RATIO] * (RATIO * RATIO * scale)
    coarse_x = np.kron(np.eye(4), at_coarse)
    coarse_x = np.stack(parts(coarse_x))
    own_y = np.transpose(basis_y.reshape(KW, n_y, cells_y), (1, 0, 2))
    along_y = np.stack(parts(own_y), 1)
    at_rows = np.transpose(basis_y[:, ::RATIO]).reshape(n_y, coarse_y, KW)
    coarse_y_table = np.stack(parts(np.tile(at_rows, (1, 1, fields_count))), 1).astype(np.float32)
    return project_x, expand_x, coarse_x, along_y, coarse_y_table


def split(values):
    high = values.astype(BF16)
    return high, (values - high.astype(F32)).astype(BF16)


def dot(a, b):
    return jnp.dot(a, b, preferred_element_type=F32)


def dot_nt(a, b):
    return lax.dot_general(a, b, NT, preferred_element_type=F32)


def body(
    sizes,
    fields_hbm, terrain, columns, tile, cells, weights,
    project_x_hbm, expand_x_hbm, coarse_x, along_y_hbm, coarse_y_hbm,
    state, coeffs,
    padded, column_rows, coarse, target, heights, heights_got, edge_rows, edge_rows_got,
    edge_columns, edge_columns_got, partial, partial_got, plane, total,
    project_x, expand_x, along_y, coarse_y_table, block_y, y_terms,
    load_sem, send_h, recv_h, send_e, recv_e, send_r, recv_r, send_p, recv_p, send_t, recv_t,
):
    n_x, n_y, variables, levels, parent_levels = sizes
    count = variables * levels
    cells_x, cells_y = terrain.shape
    tile_x, tile_y = cells_x // RATIO, cells_y // RATIO
    row_x = n_x * tile_x
    width = row_x * tile_y
    groups = tile_y // 4
    span = 4 * row_x
    records = tile.shape[1]
    top = 8
    me_x, me_y = lax.axis_index("gx"), lax.axis_index("gy")

    loads = [
        pltpu.make_async_copy(fields_hbm, padded.at[:, pl.ds(top, cells_x), :], load_sem.at[0]),
        pltpu.make_async_copy(project_x_hbm.at[me_x], project_x, load_sem.at[1]),
        pltpu.make_async_copy(expand_x_hbm.at[me_x], expand_x, load_sem.at[2]),
        pltpu.make_async_copy(along_y_hbm.at[me_y], along_y, load_sem.at[3]),
        pltpu.make_async_copy(coarse_y_hbm.at[me_y], coarse_y_table, load_sem.at[4]),
    ]
    for load in loads:
        load.start()

    edge_rows_got[...] = jnp.zeros_like(edge_rows_got)
    edge_columns_got[...] = jnp.zeros_like(edge_columns_got)
    barrier = pltpu.get_barrier_semaphore()
    for d in range(1, n_x):
        pl.semaphore_signal(
            barrier, inc=1, device_id=(lax.rem(me_x + d, n_x), me_y), device_id_type=MESH
        )
    for d in range(1, n_y):
        pl.semaphore_signal(
            barrier, inc=1, device_id=(me_x, lax.rem(me_y + d, n_y)), device_id_type=MESH
        )

    ground = terrain[pl.ds(0, tile_x, RATIO), :]
    low_bits = ground & 255
    ground = jnp.concatenate(
        [(ground - low_bits).astype(F32), low_bits.astype(F32)], axis=0
    ).astype(BF16)
    for g in range(groups):
        lane = lax.broadcasted_iota(jnp.int32, (cells_y, span), 1)
        row = lax.broadcasted_iota(jnp.int32, (cells_y, span), 0)
        pick = jnp.where(row == RATIO * (4 * g + lane // row_x), 1.0, 0.0).astype(BF16)
        both = dot(ground, pick)
        here = both[:tile_x] + both[tile_x:]
        lane = lax.broadcasted_iota(jnp.int32, (tile_x, span), 1)
        row = lax.broadcasted_iota(jnp.int32, (tile_x, span), 0)
        here = jnp.where(lane % row_x == me_x * tile_x + row, here, 0.0)
        heights[g : g + 1, :] = jnp.sum(here, axis=0, keepdims=True)

    pl.semaphore_wait(barrier, n_x + n_y - 2)
    sends_h = []
    for d in range(1, n_x):
        sends_h.append(
            pltpu.make_async_remote_copy(
                src_ref=heights,
                dst_ref=heights_got.at[d],
                send_sem=send_h.at[d],
                recv_sem=recv_h.at[d],
                device_id=(lax.rem(me_x + d, n_x), me_y),
                device_id_type=MESH,
            )
        )
        sends_h[-1].start()

    for load in loads:
        load.wait()

    edge_rows[0] = padded[:, top, :]
    edge_rows[1] = padded[:, top + cells_x - 1, :]
    lane = lax.broadcasted_iota(jnp.int32, (cells_x, cells_y), 1)
    first = jnp.zeros((cells_x, cells_y), F32)
    last = jnp.zeros((cells_x, cells_y), F32)
    for i in range(count):
        q = padded[i, top : top + cells_x, :]
        first = jnp.where(lane == i, q if i == 0 else pltpu.roll(q, i, 1), first)
        last = jnp.where(lane == i, pltpu.roll(q, i + 1, 1), last)
    edge_columns[0] = first
    edge_columns[1] = last

    def edge_copy(source, got, side, slot, device):
        return pltpu.make_async_remote_copy(
            src_ref=source.at[side],
            dst_ref=got.at[side],
            send_sem=send_e.at[slot],
            recv_sem=recv_e.at[slot],
            device_id=device,
            device_id_type=MESH,
        )

    down_x = edge_copy(edge_rows, edge_rows_got, 0, 0, (jnp.maximum(me_x - 1, 0), me_y))
    up_x = edge_copy(edge_rows, edge_rows_got, 1, 1, (jnp.minimum(me_x + 1, n_x - 1), me_y))
    down_y = edge_copy(edge_columns, edge_columns_got, 0, 2, (me_x, jnp.maximum(me_y - 1, 0)))
    up_y = edge_copy(edge_columns, edge_columns_got, 1, 3, (me_x, jnp.minimum(me_y + 1, n_y - 1)))
    has_down_x, has_up_x = me_x > 0, me_x < n_x - 1
    has_down_y, has_up_y = me_y > 0, me_y < n_y - 1
    edges = [
        (down_x, has_down_x, has_up_x),
        (up_x, has_up_x, has_down_x),
        (down_y, has_down_y, has_up_y),
        (up_y, has_up_y, has_down_y),
    ]
    for copy, out, _ in edges:
        pl.when(out)(copy.start)

    zero_block = jnp.zeros((KW, cells_y), BF16)
    for part in range(2):
        block = along_y[part]
        for q in range(4):
            block_y[part, q * KW : (q + 1) * KW, :] = jnp.concatenate(
                [block if q == j else zero_block for j in range(4)], axis=1
            )
    for g in range(count // 4):
        highs, lows = [], []
        for i in range(4 * g, 4 * g + 4):
            high, low = split(padded[i, top : top + cells_x, :])
            highs.append(high)
            lows.append(low)
        stacked = jnp.concatenate(
            [jnp.concatenate(highs, axis=1), jnp.concatenate(lows, axis=1)], axis=0
        )
        both = dot(project_x[...], stacked)
        y_terms[g * KW : (g + 1) * KW, :] = both[:KW] + both[KW:]
    high, low = split(y_terms[...])
    nest = dot_nt(high, block_y[0]) + dot_nt(low, block_y[0]) + dot_nt(high, block_y[1])

    column_rows[...] = jnp.zeros_like(column_rows)
    for v in range(variables):
        column_rows[v * 64 : v * 64 + parent_levels, :] = columns[v].astype(F32)
    packed = column_rows[...].astype(BF16)
    place = cells[...]
    place = (place % tile_y) * row_x + tile[...] * tile_x + place // tile_y
    amount = weights[...].astype(F32)
    step = 256 if width % 256 == 0 else 128

    def spread(i, carry):
        line = lax.broadcasted_iota(jnp.int32, (step, records), 0) + i * step
        matrix = jnp.zeros((step, records), F32)
        for e in range(place.shape[0]):
            matrix = matrix + jnp.where(place[e : e + 1] == line, amount[e : e + 1], 0.0)
        high, low = split(matrix)
        at = pl.ds(pl.multiple_of(i * step, step), step)
        coarse[:, at] = dot_nt(packed, high) + dot_nt(packed, low)
        return carry

    lax.fori_loop(0, width // step, spread, 0)

    for copy in sends_h:
        copy.wait()
    height = heights[...]
    for d in range(1, n_x):
        height = height + heights_got[d]
    heights[...] = height

    level = lax.broadcasted_iota(jnp.int32, (64, 128), 0)
    parent_height = jnp.where(
        level < parent_levels, (level.astype(F32) + 0.5) * (TOP / parent_levels), 1e9
    )
    chunks = span // 128
    for g in range(groups):

        def interpolate(j, carry):
            lanes = pl.ds(pl.multiple_of(j * 128, 128), 128)
            at = pl.ds(pl.multiple_of(g * span + j * 128, 128), 128)
            h = heights[g : g + 1, lanes]
            spacing = (TOP - h) / levels
            inverse = 1.0 / spacing
            base = h * inverse
            scaled = parent_height * inverse
            rows = [[] for _ in range(variables)]
            for k in range(levels):
                hat = jnp.maximum(0.0, 1.0 - jnp.abs((base + (k + 0.5)) - scaled))
                norm = 1.0 / jnp.sum(hat, axis=0, keepdims=True)
                for v in range(variables):
                    value = coarse[v * 64 : (v + 1) * 64, at]
                    rows[v].append(jnp.sum(hat * value, axis=0, keepdims=True) * norm)
            for v in range(variables):
                target[g * KW + v * levels : g * KW + (v + 1) * levels, lanes] = jnp.concatenate(
                    rows[v], axis=0
                )
            target[g * KW + count : (g + 1) * KW, lanes] = jnp.zeros((KW - count, 128), F32)
            return carry

        lax.fori_loop(0, chunks, interpolate, 0)

    high, low = split(target[...])
    along_x = dot_nt(coarse_x[0], high) + dot_nt(coarse_x[0], low) + dot_nt(coarse_x[1], high)
    along_x = jnp.concatenate([along_x[r * KW : (r + 1) * KW] for r in range(4)], axis=1)
    high, low = split(along_x)
    lane = lax.broadcasted_iota(jnp.int32, (KW, count * KW), 1)
    row = lax.broadcasted_iota(jnp.int32, (KW, count * KW), 0)
    own = lane // KW == row
    spread_y = []
    for part in range(2):
        blocks = []
        for r in range(4):
            for g in range(groups):
                values = coarse_y_table[part, 4 * g + r : 4 * g + r + 1, :]
                blocks.append(jnp.where(own, values, 0.0).astype(BF16))
        spread_y.append(jnp.concatenate(blocks, axis=0))
    wanted = dot(high, spread_y[0]) + dot(low, spread_y[0]) + dot(high, spread_y[1])

    lines = count // 4 * KW
    difference = [
        nest[g * KW : (g + 1) * KW] - wanted[:, g * 128 : (g + 1) * 128]
        for g in range(count // 4)
    ]
    difference = jnp.concatenate(difference, axis=0)
    piece = partial.shape[1]
    if n_x * piece != lines:
        difference = jnp.concatenate(
            [difference, jnp.zeros((n_x * piece - lines, 128), F32)], axis=0
        )
    for i in range(n_x):
        partial[i] = difference[i * piece : (i + 1) * piece]
    sends_r = []
    for d in range(1, n_x):
        to = lax.rem(me_x + d, n_x)
        sends_r.append(
            pltpu.make_async_remote_copy(
                src_ref=partial.at[to],
                dst_ref=partial_got.at[d],
                send_sem=send_r.at[d],
                recv_sem=recv_r.at[d],
                device_id=(to, me_y),
                device_id_type=MESH,
            )
        )
        sends_r[-1].start()

    for copy, out, arrives in edges:
        pl.when(out)(copy.wait_send)
        pl.when(arrives)(copy.wait_recv)
    padded[:, top + cells_x, :] = edge_rows_got[0]
    padded[:, top - 1, :] = edge_rows_got[1]
    metric = TOP / (TOP - terrain[...].astype(F32))
    metric = 0.1 * (metric * metric)

    def advance(k, carry):
        wind_x = 0.05 * padded[k, top : top + cells_x, :]
        wind_y = 0.05 * padded[levels + k, top : top + cells_x, :]
        above_k = jnp.minimum(k + 1, levels - 1)
        below_k = jnp.maximum(k - 1, 0)
        lane = lax.broadcasted_iota(jnp.int32, (cells_x, cells_y), 1)
        for v in range(variables):
            i = v * levels + k
            q = padded[i, top : top + cells_x, :]
            east = padded[i, top + 1 : top + 1 + cells_x, :]
            west = padded[i, top - 1 : top - 1 + cells_x, :]
            north = jnp.where(
                lane == cells_y - 1,
                pltpu.roll(edge_columns_got[0], cells_y - 1 - i, 1),
                pltpu.roll(q, cells_y - 1, 1),
            )
            south = jnp.where(
                lane == 0,
                pltpu.roll(edge_columns_got[1], lax.rem(cells_y - i, cells_y), 1),
                pltpu.roll(q, 1, 1),
            )
            above = padded[v * levels + above_k, top : top + cells_x, :]
            below = padded[v * levels + below_k, top : top + cells_x, :]
            transport = wind_x * (east - west) + wind_y * (north - south)
            diffusion = 0.1 * ((east + west) + (north + south) - 4.0 * q)
            mixing = metric * ((above + below) - 2.0 * q)
            state[i] = q - transport + diffusion + mixing
        return carry

    half_levels = levels // 2
    lax.fori_loop(0, half_levels, advance, 0)

    for copy in sends_r:
        copy.wait()
    mine = partial[me_x]
    for d in range(1, n_x):
        mine = mine + partial_got[d]
    plane[me_y] = mine
    sends_p = []
    for d in range(1, n_y):
        sends_p.append(
            pltpu.make_async_remote_copy(
                src_ref=plane.at[me_y],
                dst_ref=plane.at[me_y],
                send_sem=send_p.at[d],
                recv_sem=recv_p.at[d],
                device_id=(me_x, lax.rem(me_y + d, n_y)),
                device_id_type=MESH,
            )
        )
        sends_p[-1].start()
    lax.fori_loop(half_levels, levels, advance, 0)
    for copy in sends_p:
        copy.wait()
    mine = plane[0]
    for j in range(1, n_y):
        mine = mine + plane[j]
    total[me_x] = mine
    sends_t = []
    for d in range(1, n_x):
        sends_t.append(
            pltpu.make_async_remote_copy(
                src_ref=total.at[me_x],
                dst_ref=total.at[me_x],
                send_sem=send_t.at[d],
                recv_sem=recv_t.at[d],
                device_id=(lax.rem(me_x + d, n_x), me_y),
                device_id_type=MESH,
            )
        )
        sends_t[-1].start()
    for copy in sends_t:
        copy.wait()

    summed = jnp.concatenate([total[i] for i in range(n_x)], axis=0)[:lines]
    for i in range(count):
        g, q = i // 4, i % 4
        coeffs[i] = summed[g * KW : (g + 1) * KW, q * KW : (q + 1) * KW]

    high, low = split(summed)
    along = dot(high, block_y[0]) + dot(low, block_y[0]) + dot(high, block_y[1])
    for g in range(count // 4):
        high, low = split(along[g * KW : (g + 1) * KW])
        modes = dot(expand_x[...], jnp.concatenate([high, high, low], axis=0))
        for q in range(4):
            i = 4 * g + q
            state[i] = state[i] - modes[:, q * cells_y : (q + 1) * cells_y]


def per_device(sizes, fields, terrain, parent_columns, record_tile, record_cells, record_weights):
    n_x, n_y = sizes
    variables, levels, cells_x, cells_y = fields.shape
    parent_levels, records = parent_columns.shape[1:]
    count = variables * levels
    tile_x, tile_y = cells_x // RATIO, cells_y // RATIO
    row_x = n_x * tile_x
    width = row_x * tile_y
    groups = tile_y // 4
    lines = count // 4 * KW
    piece = -(-lines // (8 * n_x)) * 8
    project_x, expand_x, coarse_x, along_y, coarse_y_table = tables(
        n_x, n_y, cells_x, cells_y, count
    )
    vmem = pl.BlockSpec(memory_space=pltpu.VMEM)
    hbm = pl.BlockSpec(memory_space=pl.ANY)
    dma = pltpu.SemaphoreType.DMA
    state, coeffs = pl.pallas_call(
        functools.partial(body, (n_x, n_y, variables, levels, parent_levels)),
        out_shape=(
            jax.ShapeDtypeStruct((count, cells_x, cells_y), F32),
            jax.ShapeDtypeStruct((count, KW, KW), F32),
        ),
        in_specs=[hbm, vmem, vmem, vmem, vmem, vmem, hbm, hbm, vmem, hbm, hbm],
        out_specs=(vmem, vmem),
        scratch_shapes=[
            pltpu.VMEM((count, cells_x + 16, cells_y), F32),
            pltpu.VMEM((variables * 64, records), F32),
            pltpu.VMEM((variables * 64, width), F32),
            pltpu.VMEM((groups * KW, 4 * row_x), F32),
            pltpu.VMEM((groups, 4 * row_x), F32),
            pltpu.VMEM((n_x, groups, 4 * row_x), F32),
            pltpu.VMEM((2, count, cells_y), F32),
            pltpu.VMEM((2, count, cells_y), F32),
            pltpu.VMEM((2, cells_x, cells_y), F32),
            pltpu.VMEM((2, cells_x, cells_y), F32),
            pltpu.VMEM((n_x, piece, 128), F32),
            pltpu.VMEM((n_x, piece, 128), F32),
            pltpu.VMEM((n_y, piece, 128), F32),
            pltpu.VMEM((n_x, piece, 128), F32),
            pltpu.VMEM(project_x.shape[1:], BF16),
            pltpu.VMEM(expand_x.shape[1:], BF16),
            pltpu.VMEM(along_y.shape[1:], BF16),
            pltpu.VMEM(coarse_y_table.shape[1:], F32),
            pltpu.VMEM((2, 4 * KW, 4 * cells_y), BF16),
            pltpu.VMEM((lines, 4 * cells_y), F32),
            dma((5,)),
            dma((n_x,)), dma((n_x,)),
            dma((4,)), dma((4,)),
            dma((n_x,)), dma((n_x,)),
            dma((n_y,)), dma((n_y,)),
            dma((n_x,)), dma((n_x,)),
        ],
        compiler_params=pltpu.CompilerParams(
            collective_id=0, has_side_effects=True, vmem_limit_bytes=48 * 1024 * 1024
        ),
        name="nudge",
    )(
        fields.reshape(count, cells_x, cells_y), terrain, parent_columns,
        record_tile.T, record_cells.T, record_weights.T,
        jnp.asarray(project_x), jnp.asarray(expand_x), jnp.asarray(coarse_x),
        jnp.asarray(along_y), jnp.asarray(coarse_y_table),
    )
    return state.reshape(fields.shape), coeffs.reshape(variables, levels, KW, KW)


def solution(mesh):
    sizes = (mesh.shape["gx"], mesh.shape["gy"])
    return jax.shard_map(
        functools.partial(per_device, sizes),
        mesh=mesh,
        in_specs=(
            P(None, None, "gx", "gy"),
            P("gx", "gy"),
            P(None, None, ("gx", "gy")),
            P(("gx", "gy"), None),
            P(("gx", "gy"), None),
            P(("gx", "gy"), None),
        ),
        out_specs=(P(None, None, "gx", "gy"), P()),
        check_vma=False,
    )
```

profile of v0, /device:TPU:0, one launch (start us, length us, event | category | flops | bytes accessed | tf_op | source)
XLA Modules:
  0.0 35.9 jit_solution(11456239980753327360)
XLA Ops:
  0.6 0.0 copy-start
  0.6 1.3 %copy-done = f32[3,8,96,128]{3,2,1,0:T(8,128)S(1)} copy-done((f32[3,8,96,128]{3,2,1,0:T(8,128)S(1)}, f32[3,8,96,128]{3,2,1,0:T(8,128)}, u32[]{:S(2)}) %copy-start) | copy-done | bytes 1179672
  1.9 0.0 copy-start.1
  1.9 1.0 %copy-done.1 = f32[4,2,16,768]{3,2,1,0:T(8,128)S(1)} copy-done((f32[4,2,16,768]{3,2,1,0:T(8,128)S(1)}, f32[4,2,16,768]{3,2,1,0:T(8,128)}, u32[]{:S(2)}) %copy-start.1) | copy-done | bytes 393240
  2.9 0.9 %copy-done.2 = bf16[8,64,192]{2,1,0:T(8,128)(2,1)S(1)} copy-done((bf16[8,64,192]{2,1,0:T(8,128)(2,1)S(1)}, bf16[8,64,192]{2,1,0:T(8,128)(2,1)}, u32[]{:S(2)}) %copy-start.2) | copy-done | bytes 196632
  3.9 0.0 copy-start.3
  3.9 0.9 %copy-done.3 = bf16[2,128,384]{2,1,0:T(8,128)(2,1)S(1)} copy-done((bf16[2,128,384]{2,1,0:T(8,128)(2,1)S(1)}, bf16[2,128,384]{2,1,0:T(8,128)(2,1)}, u32[]{:S(2)}) %copy-start.3) | copy-done | bytes 196632
  4.8 0.0 copy-start.4
  4.8 0.9 %copy-done.4 = bf16[8,96,96]{2,1,0:T(8,128)(2,1)S(1)} copy-done((bf16[8,96,96]{2,1,0:T(8,128)(2,1)S(1)}, bf16[8,96,96]{2,1,0:T(8,128)(2,1)}, u32[]{:S(2)}) %copy-start.4) | copy-done | bytes 147480
  5.7 0.0 copy-start.5
  5.7 0.9 %copy-done.5 = bf16[3,60,384]{2,1,0:T(8,128)(2,1)S(1)} copy-done((bf16[3,60,384]{2,1,0:T(8,128)(2,1)S(1)}, bf16[3,60,384]{2,1,0:T(8,128)(2,1)}, u32[]{:S(2)}) %copy-start.5) | copy-done | bytes 138264
  6.6 0.0 copy-start.6
  6.6 0.8 %copy-done.6 = bf16[4,2,32,128]{3,2,1,0:T(8,128)(2,1)S(1)} copy-done((bf16[4,2,32,128]{3,2,1,0:T(8,128)(2,1)S(1)}, bf16[4,2,32,128]{3,2,1,0:T(8,128)(2,1)}, u32[]{:S(2)}) %copy-start.6) | copy-done | bytes 65560
  7.5 0.0 copy-start.7
  7.5 0.8 %copy-done.7 = s32[96,128]{1,0:T(8,128)S(1)} copy-done((s32[96,128]{1,0:T(8,128)S(1)}, s32[96,128]{1,0:T(8,128)}, u32[]{:S(2)}) %copy-start.7) | copy-done | bytes 49176
  8.3 0.0 copy-start.8
  8.3 0.7 %copy-done.8 = s32[384,4]{0,1:T(4,128)S(1)} copy-done((s32[384,4]{0,1:T(4,128)S(1)}, s32[384,4]{0,1:T(4,128)}, u32[]{:S(2)}) %copy-start.8) | copy-done | bytes 6168
  8.9 0.0 copy-start.9
  8.9 0.7 %copy-done.9 = bf16[384,4]{0,1:T(4,128)(2,1)S(1)} copy-done((bf16[384,4]{0,1:T(4,128)(2,1)S(1)}, bf16[384,4]{0,1:T(4,128)(2,1)}, u32[]{:S(2)}) %copy-start.9) | copy-done | bytes 3096
  9.6 0.0 copy-start.10
  9.6 0.7 %copy-done.10 = s32[384,1]{0,1:T(1,128)S(1)} copy-done((s32[384,1]{0,1:T(1,128)S(1)}, s32[384,1]{0,1:T(1,128)}, u32[]{:S(2)}) %copy-start.10) | copy-done | bytes 1560
  10.3 23.8 %nudge.1 = (f32[24,96,128]{2,1,0:T(8,128)S(1)}, f32[24,32,32]{2,1,0:T(8,128)S(1)}) custom-call(f32[24,96,128]{2,1,0:T(8,128)S(1)} %bitcast.6, s32[96,128]{1,0:T(8,128)S(1)} %copy-done.7, bf16[3,60,384]{2,1,0:T(8,128)(2,1)S(1)} %copy-done.5, s32[1,384]{1,0:T(1,128)S(1)} %bitcast.11, s32[4,384]{1,0:T(4,128)S(1)} %bitcast.9, bf16[4,384]{1,0:T(4,128)(2,1)S(1)} %bitcast.10, ...), custom_call_target="tpu_custom_call" | custom-call | tf_op jit(solution)/shard_map/nudge/pallas_call | solution.py:433
  34.2 1.0 %copy.15 = f32[3,8,96,128]{3,2,1,0:T(8,128)} copy(f32[3,8,96,128]{3,2,1,0:T(8,128)S(1)} %bitcast.7) | data formatting | bytes 2359296
  35.2 0.7 %copy.16 = f32[3,8,32,32]{3,2,1,0:T(8,128)} copy(f32[3,8,32,32]{3,2,1,0:T(8,128)S(1)} %bitcast.8) | data formatting | bytes 196608
  (1 shorter events, 0.0 us)
Async XLA Ops:
  0.6 1.3 %copy-start = (f32[3,8,96,128]{3,2,1,0:T(8,128)S(1)}, f32[3,8,96,128]{3,2,1,0:T(8,128)}, u32[]{:S(2)}) copy-start(f32[3,8,96,128]{3,2,1,0:T(8,128)} %param.11) | copy-start | bytes 3538948
  1.9 1.0 %copy-start.1 = (f32[4,2,16,768]{3,2,1,0:T(8,128)S(1)}, f32[4,2,16,768]{3,2,1,0:T(8,128)}, u32[]{:S(2)}) copy-start(f32[4,2,16,768]{3,2,1,0:T(8,128)} %constant.14.clone.coarse_y_hbm) | copy-start | bytes 1179652
  2.9 0.9 %copy-start.2 = (bf16[8,64,192]{2,1,0:T(8,128)(2,1)S(1)}, bf16[8,64,192]{2,1,0:T(8,128)(2,1)}, u32[]{:S(2)}) copy-start(bf16[8,64,192]{2,1,0:T(8,128)(2,1)} %constant.10.clone.project_x_hbm) | copy-start | bytes 589828
  3.9 0.9 %copy-start.3 = (bf16[2,128,384]{2,1,0:T(8,128)(2,1)S(1)}, bf16[2,128,384]{2,1,0:T(8,128)(2,1)}, u32[]{:S(2)}) copy-start(bf16[2,128,384]{2,1,0:T(8,128)(2,1)} %constant.12.clone.coarse_x) | copy-start | bytes 589828
  4.8 0.9 %copy-start.4 = (bf16[8,96,96]{2,1,0:T(8,128)(2,1)S(1)}, bf16[8,96,96]{2,1,0:T(8,128)(2,1)}, u32[]{:S(2)}) copy-start(bf16[8,96,96]{2,1,0:T(8,128)(2,1)} %constant.11.clone.expand_x_hbm) | copy-start | bytes 442372
  5.7 0.9 %copy-start.5 = (bf16[3,60,384]{2,1,0:T(8,128)(2,1)S(1)}, bf16[3,60,384]{2,1,0:T(8,128)(2,1)}, u32[]{:S(2)}) copy-start(bf16[3,60,384]{2,1,0:T(8,128)(2,1)} %columns.1) | copy-start | bytes 414724
  6.6 0.8 %copy-start.6 = (bf16[4,2,32,128]{3,2,1,0:T(8,128)(2,1)S(1)}, bf16[4,2,32,128]{3,2,1,0:T(8,128)(2,1)}, u32[]{:S(2)}) copy-start(bf16[4,2,32,128]{3,2,1,0:T(8,128)(2,1)} %constant.13.clone.along_y_hbm) | copy-start | bytes 196612
  7.5 0.8 %copy-start.7 = (s32[96,128]{1,0:T(8,128)S(1)}, s32[96,128]{1,0:T(8,128)}, u32[]{:S(2)}) copy-start(s32[96,128]{1,0:T(8,128)} %terrain.1) | copy-start | bytes 147460
  8.3 0.7 %copy-start.8 = (s32[384,4]{0,1:T(4,128)S(1)}, s32[384,4]{0,1:T(4,128)}, u32[]{:S(2)}) copy-start(s32[384,4]{0,1:T(4,128)} %param.15) | copy-start | bytes 18436
  8.9 0.7 %copy-start.9 = (bf16[384,4]{0,1:T(4,128)(2,1)S(1)}, bf16[384,4]{0,1:T(4,128)(2,1)}, u32[]{:S(2)}) copy-start(bf16[384,4]{0,1:T(4,128)(2,1)} %param.16) | copy-start | bytes 9220
  9.6 0.7 %copy-start.10 = (s32[384,1]{0,1:T(1,128)S(1)}, s32[384,1]{0,1:T(1,128)}, u32[]{:S(2)}) copy-start(s32[384,1]{0,1:T(1,128)} %param.14) | copy-start | bytes 4612
where the time goes:
time: 36.4 us; the launch traced here: 35.9 us
  Pallas kernels  23.8 us (65%)
  local copies, waits for them, and re-layouts  11.4 us (31%)
  between operations  0.66 us (2%)
    pallas_call x1, Pallas kernels, per_device(): pl.pallas_call(functools.partial(body, (n_x, n_y, variables, levels, pare...  23.8 us
    unnamed x24, local copies, waits for them, and re-layouts  11.4 us

commit v1 on v0

--- a/solution.py
+++ b/solution.py
@@ -78,13 +78,14 @@
 
 def body(
     sizes,
-    fields_hbm, terrain, columns, tile, cells, weights,
-    project_x_hbm, expand_x_hbm, coarse_x, along_y_hbm, coarse_y_hbm,
-    state, coeffs,
+    fields_hbm, terrain_hbm, columns_hbm, tile_hbm, cells_hbm, weights_hbm,
+    project_x_hbm, coarse_x_hbm, along_y_hbm, coarse_y_hbm,
+    state_hbm, total_hbm,
+    state, terrain, columns, tile, cells, weights, coarse_x,
     padded, column_rows, coarse, target, heights, heights_got, edge_rows, edge_rows_got,
     edge_columns, edge_columns_got, partial, partial_got, plane, total,
-    project_x, expand_x, along_y, coarse_y_table, block_y, y_terms,
-    load_sem, send_h, recv_h, send_e, recv_e, send_r, recv_r, send_p, recv_p, send_t, recv_t,
+    project_x, along_y, coarse_y_table, y_terms,
+    load_sem, store_sem, send_h, recv_h, send_e, recv_e, send_r, recv_r, send_p, recv_p, send_t, recv_t,
 ):
     n_x, n_y, variables, levels, parent_levels = sizes
     count = variables * levels
@@ -101,10 +102,19 @@
     loads = [
         pltpu.make_async_copy(fields_hbm, padded.at[:, pl.ds(top, cells_x), :], load_sem.at[0]),
         pltpu.make_async_copy(project_x_hbm.at[me_x], project_x, load_sem.at[1]),
-        pltpu.make_async_copy(expand_x_hbm.at[me_x], expand_x, load_sem.at[2]),
         pltpu.make_async_copy(along_y_hbm.at[me_y], along_y, load_sem.at[3]),
         pltpu.make_async_copy(coarse_y_hbm.at[me_y], coarse_y_table, load_sem.at[4]),
+        pltpu.make_async_copy(coarse_x_hbm, coarse_x, load_sem.at[5]),
     ]
+    early = [
+        pltpu.make_async_copy(terrain_hbm, terrain, load_sem.at[6]),
+        pltpu.make_async_copy(columns_hbm, columns, load_sem.at[7]),
+        pltpu.make_async_copy(tile_hbm, tile, load_sem.at[8]),
+        pltpu.make_async_copy(cells_hbm, cells, load_sem.at[9]),
+        pltpu.make_async_copy(weights_hbm, weights, load_sem.at[10]),
+    ]
+    for load in early:
+        load.start()
     for load in loads:
         load.start()
 
@@ -120,21 +130,44 @@
             barrier, inc=1, device_id=(me_x, lax.rem(me_y + d, n_y)), device_id_type=MESH
         )
 
+    early[0].wait()
     ground = terrain[pl.ds(0, tile_x, RATIO), :]
     low_bits = ground & 255
     ground = jnp.concatenate(
         [(ground - low_bits).astype(F32), low_bits.astype(F32)], axis=0
     ).astype(BF16)
     for g in range(groups):
-        lane = lax.broadcasted_iota(jnp.int32, (cells_y, span), 1)
+        lane = lax.broadcasted_iota(jnp.int32, (1, span), 1)
         row = lax.broadcasted_iota(jnp.int32, (cells_y, span), 0)
         pick = jnp.where(row == RATIO * (4 * g + lane // row_x), 1.0, 0.0).astype(BF16)
         both = dot(ground, pick)
         here = both[:tile_x] + both[tile_x:]
-        lane = lax.broadcasted_iota(jnp.int32, (tile_x, span), 1)
         row = lax.broadcasted_iota(jnp.int32, (tile_x, span), 0)
-        here = jnp.where(lane % row_x == me_x * tile_x + row, here, 0.0)
+        here = jnp.where(lane % row_x - me_x * tile_x == row, here, 0.0)
         heights[g : g + 1, :] = jnp.sum(here, axis=0, keepdims=True)
+
+    for load in early[1:]:
+        load.wait()
+    column_rows[...] = jnp.zeros_like(column_rows)
+    for v in range(variables):
+        column_rows[v * 64 : v * 64 + parent_levels, :] = columns[v].astype(F32)
+    packed = column_rows[...].astype(BF16)
+    place = cells[...]
+    place = (place % tile_y) * row_x + tile[...] * tile_x + place // tile_y
+    amount = weights[...].astype(F32)
+    step = 256 if width % 256 == 0 else 128
+
+    def spread(i, carry):
+        line = lax.broadcasted_iota(jnp.int32, (step, records), 0) + i * step
+        matrix = jnp.zeros((step, records), F32)
+        for e in range(place.shape[0]):
+            matrix = matrix + jnp.where(place[e : e + 1] == line, amount[e : e + 1], 0.0)
+        high, low = split(matrix)
+        at = pl.ds(pl.multiple_of(i * step, step), step)
+        coarse[:, at] = dot_nt(packed, high) + dot_nt(packed, low)
+        return carry
+
+    lax.fori_loop(0, width // step, spread, 0)
 
     pl.semaphore_wait(barrier, n_x + n_y - 2)
     sends_h = []
@@ -154,50 +187,7 @@
     for load in loads:
         load.wait()
 
-    edge_rows[0] = padded[:, top, :]
-    edge_rows[1] = padded[:, top + cells_x - 1, :]
-    lane = lax.broadcasted_iota(jnp.int32, (cells_x, cells_y), 1)
-    first = jnp.zeros((cells_x, cells_y), F32)
-    last = jnp.zeros((cells_x, cells_y), F32)
-    for i in range(count):
-        q = padded[i, top : top + cells_x, :]
-        first = jnp.where(lane == i, q if i == 0 else pltpu.roll(q, i, 1), first)
-        last = jnp.where(lane == i, pltpu.roll(q, i + 1, 1), last)
-    edge_columns[0] = first
-    edge_columns[1] = last
-
-    def edge_copy(source, got, side, slot, device):
-        return pltpu.make_async_remote_copy(
-            src_ref=source.at[side],
-            dst_ref=got.at[side],
-            send_sem=send_e.at[slot],
-            recv_sem=recv_e.at[slot],
-            device_id=device,
-            device_id_type=MESH,
-        )
-
-    down_x = edge_copy(edge_rows, edge_rows_got, 0, 0, (jnp.maximum(me_x - 1, 0), me_y))
-    up_x = edge_copy(edge_rows, edge_rows_got, 1, 1, (jnp.minimum(me_x + 1, n_x - 1), me_y))
-    down_y = edge_copy(edge_columns, edge_columns_got, 0, 2, (me_x, jnp.maximum(me_y - 1, 0)))
-    up_y = edge_copy(edge_columns, edge_columns_got, 1, 3, (me_x, jnp.minimum(me_y + 1, n_y - 1)))
-    has_down_x, has_up_x = me_x > 0, me_x < n_x - 1
-    has_down_y, has_up_y = me_y > 0, me_y < n_y - 1
-    edges = [
-        (down_x, has_down_x, has_up_x),
-        (up_x, has_up_x, has_down_x),
-        (down_y, has_down_y, has_up_y),
-        (up_y, has_up_y, has_down_y),
-    ]
-    for copy, out, _ in edges:
-        pl.when(out)(copy.start)
-
-    zero_block = jnp.zeros((KW, cells_y), BF16)
-    for part in range(2):
-        block = along_y[part]
-        for q in range(4):
-            block_y[part, q * KW : (q + 1) * KW, :] = jnp.concatenate(
-                [block if q == j else zero_block for j in range(4)], axis=1
-            )
+    block_y = [diagonal(along_y[part]) for part in range(2)]
     for g in range(count // 4):
         highs, lows = [], []
         for i in range(4 * g, 4 * g + 4):
@@ -212,26 +202,17 @@
     high, low = split(y_terms[...])
     nest = dot_nt(high, block_y[0]) + dot_nt(low, block_y[0]) + dot_nt(high, block_y[1])
 
-    column_rows[...] = jnp.zeros_like(column_rows)
-    for v in range(variables):
-        column_rows[v * 64 : v * 64 + parent_levels, :] = columns[v].astype(F32)
-    packed = column_rows[...].astype(BF16)
-    place = cells[...]
-    place = (place % tile_y) * row_x + tile[...] * tile_x + place // tile_y
-    amount = weights[...].astype(F32)
-    step = 256 if width % 256 == 0 else 128
-
-    def spread(i, carry):
-        line = lax.broadcasted_iota(jnp.int32, (step, records), 0) + i * step
-        matrix = jnp.zeros((step, records), F32)
-        for e in range(place.shape[0]):
-            matrix = matrix + jnp.where(place[e : e + 1] == line, amount[e : e + 1], 0.0)
-        high, low = split(matrix)
-        at = pl.ds(pl.multiple_of(i * step, step), step)
-        coarse[:, at] = dot_nt(packed, high) + dot_nt(packed, low)
-        return carry
-
-    lax.fori_loop(0, width // step, spread, 0)
+    lane = lax.broadcasted_iota(jnp.int32, (KW, count * KW), 1)
+    row = lax.broadcasted_iota(jnp.int32, (KW, count * KW), 0)
+    own = lane // KW == row
+    spread_y = []
+    for part in range(2):
+        blocks = []
+        for r in range(4):
+            for g in range(groups):
+                values = coarse_y_table[part, 4 * g + r : 4 * g + r + 1, :]
+                blocks.append(jnp.where(own, values, 0.0).astype(BF16))
+        spread_y.append(jnp.concatenate(blocks, axis=0))
 
     for copy in sends_h:
         copy.wait()
@@ -275,17 +256,6 @@
     along_x = dot_nt(coarse_x[0], high) + dot_nt(coarse_x[0], low) + dot_nt(coarse_x[1], high)
     along_x = jnp.concatenate([along_x[r * KW : (r + 1) * KW] for r in range(4)], axis=1)
     high, low = split(along_x)
-    lane = lax.broadcasted_iota(jnp.int32, (KW, count * KW), 1)
-    row = lax.broadcasted_iota(jnp.int32, (KW, count * KW), 0)
-    own = lane // KW == row
-    spread_y = []
-    for part in range(2):
-        blocks = []
-        for r in range(4):
-            for g in range(groups):
-                values = coarse_y_table[part, 4 * g + r : 4 * g + r + 1, :]
-                blocks.append(jnp.where(own, values, 0.0).astype(BF16))
-        spread_y.append(jnp.concatenate(blocks, axis=0))
     wanted = dot(high, spread_y[0]) + dot(low, spread_y[0]) + dot(high, spread_y[1])
 
     lines = count // 4 * KW
@@ -316,11 +286,43 @@
         )
         sends_r[-1].start()
 
-    for copy, out, arrives in edges:
-        pl.when(out)(copy.wait_send)
-        pl.when(arrives)(copy.wait_recv)
-    padded[:, top + cells_x, :] = edge_rows_got[0]
-    padded[:, top - 1, :] = edge_rows_got[1]
+    edge_rows[0] = padded[:, top, :]
+    edge_rows[1] = padded[:, top + cells_x - 1, :]
+    lane = lax.broadcasted_iota(jnp.int32, (cells_x, cells_y), 1)
+    first = jnp.zeros((cells_x, cells_y), F32)
+    last = jnp.zeros((cells_x, cells_y), F32)
+    for i in range(count):
+        q = padded[i, top : top + cells_x, :]
+        first = jnp.where(lane == i, q if i == 0 else pltpu.roll(q, i, 1), first)
+        last = jnp.where(lane == i, pltpu.roll(q, i + 1, 1), last)
+    edge_columns[0] = first
+    edge_columns[1] = last
+
+    def edge_copy(source, got, side, slot, device):
+        return pltpu.make_async_remote_copy(
+            src_ref=source.at[side],
+            dst_ref=got.at[side],
+            send_sem=send_e.at[slot],
+            recv_sem=recv_e.at[slot],
+            device_id=device,
+            device_id_type=MESH,
+        )
+
+    down_x = edge_copy(edge_rows, edge_rows_got, 0, 0, (jnp.maximum(me_x - 1, 0), me_y))
+    up_x = edge_copy(edge_rows, edge_rows_got, 1, 1, (jnp.minimum(me_x + 1, n_x - 1), me_y))
+    down_y = edge_copy(edge_columns, edge_columns_got, 0, 2, (me_x, jnp.maximum(me_y - 1, 0)))
+    up_y = edge_copy(edge_columns, edge_columns_got, 1, 3, (me_x, jnp.minimum(me_y + 1, n_y - 1)))
+    has_down_x, has_up_x = me_x > 0, me_x < n_x - 1
+    has_down_y, has_up_y = me_y > 0, me_y < n_y - 1
+    edges = [
+        (down_x, has_down_x, has_up_x),
+        (up_x, has_up_x, has_down_x),
+        (down_y, has_down_y, has_up_y),
+        (up_y, has_up_y, has_down_y),
+    ]
+    for copy, out, _ in edges:
+        pl.when(out)(copy.start)
+
     metric = TOP / (TOP - terrain[...].astype(F32))
     metric = 0.1 * (metric * metric)
 
@@ -354,8 +356,6 @@
         return carry
 
     half_levels = levels // 2
-    lax.fori_loop(0, half_levels, advance, 0)
-
     for copy in sends_r:
         copy.wait()
     mine = partial[me_x]
@@ -375,7 +375,24 @@
             )
         )
         sends_p[-1].start()
-    lax.fori_loop(half_levels, levels, advance, 0)
+    for copy, out, arrives in edges:
+        pl.when(out)(copy.wait_send)
+        pl.when(arrives)(copy.wait_recv)
+    padded[:, top + cells_x, :] = edge_rows_got[0]
+    padded[:, top - 1, :] = edge_rows_got[1]
+
+    lax.fori_loop(0, half_levels, advance, 0)
+    stores = []
+    for half in range(2):
+        for v in range(variables):
+            block = pl.ds(v * levels + half * half_levels, half_levels)
+            stores.append(
+                pltpu.make_async_copy(
+                    state.at[block], state_hbm.at[block], store_sem.at[half * variables + v]
+                )
+            )
+    for store in stores[:variables]:
+        store.start()
     for copy in sends_p:
         copy.wait()
     mine = plane[0]
@@ -395,22 +412,74 @@
             )
         )
         sends_t[-1].start()
+    lax.fori_loop(half_levels, levels, advance, 0)
+    for store in stores[variables:]:
+        store.start()
     for copy in sends_t:
         copy.wait()
 
+    stores.append(pltpu.make_async_copy(total, total_hbm, store_sem.at[2 * variables]))
+    stores[-1].start()
+    for store in stores:
+        store.wait()
+
+
+def diagonal(block):
+    empty = jnp.zeros_like(block)
+    return jnp.concatenate(
+        [
+            jnp.concatenate([block if q == j else empty for j in range(4)], axis=1)
+            for q in range(4)
+        ],
+        axis=0,
+    )
+
+
+def finish(
+    partial_hbm, total_hbm, expand_x_hbm, along_y_hbm,
+    state_hbm, coeffs_hbm,
+    state, total, expand_x, along_y, coeffs, load_sem, store_sem,
+):
+    count, _, cells_y = state.shape
+    n_x, piece = total.shape[:2]
+    lines = count // 4 * KW
+    loads = [
+        pltpu.make_async_copy(total_hbm, total, load_sem.at[0]),
+        pltpu.make_async_copy(along_y_hbm.at[lax.axis_index("gy")], along_y, load_sem.at[1]),
+        pltpu.make_async_copy(expand_x_hbm.at[lax.axis_index("gx")], expand_x, load_sem.at[2]),
+    ]
+    for g in range(count // 4):
+        block = pl.ds(4 * g, 4)
+        loads.append(
+            pltpu.make_async_copy(partial_hbm.at[block], state.at[block], load_sem.at[3 + g])
+        )
+    for load in loads:
+        load.start()
+    for load in loads[:3]:
+        load.wait()
     summed = jnp.concatenate([total[i] for i in range(n_x)], axis=0)[:lines]
     for i in range(count):
         g, q = i // 4, i % 4
         coeffs[i] = summed[g * KW : (g + 1) * KW, q * KW : (q + 1) * KW]
-
+    stores = [pltpu.make_async_copy(coeffs, coeffs_hbm, store_sem.at[0])]
+    stores[0].start()
     high, low = split(summed)
-    along = dot(high, block_y[0]) + dot(low, block_y[0]) + dot(high, block_y[1])
+    block = diagonal(along_y[0])
+    along = dot(high, block) + dot(low, block) + dot(high, diagonal(along_y[1]))
     for g in range(count // 4):
         high, low = split(along[g * KW : (g + 1) * KW])
         modes = dot(expand_x[...], jnp.concatenate([high, high, low], axis=0))
+        loads[3 + g].wait()
         for q in range(4):
             i = 4 * g + q
             state[i] = state[i] - modes[:, q * cells_y : (q + 1) * cells_y]
+        block = pl.ds(4 * g, 4)
+        stores.append(
+            pltpu.make_async_copy(state.at[block], state_hbm.at[block], store_sem.at[g + 1])
+        )
+        stores[-1].start()
+    for store in stores:
+        store.wait()
 
 
 def per_device(sizes, fields, terrain, parent_columns, record_tile, record_cells, record_weights):
@@ -427,18 +496,25 @@
     project_x, expand_x, coarse_x, along_y, coarse_y_table = tables(
         n_x, n_y, cells_x, cells_y, count
     )
-    vmem = pl.BlockSpec(memory_space=pltpu.VMEM)
-    hbm = pl.BlockSpec(memory_space=pl.ANY)
+    along_y = jnp.asarray(along_y)
+    hbm = pl.BlockSpec(memory_space=pltpu.HBM)
     dma = pltpu.SemaphoreType.DMA
-    state, coeffs = pl.pallas_call(
+    partial_state, summed = pl.pallas_call(
         functools.partial(body, (n_x, n_y, variables, levels, parent_levels)),
         out_shape=(
             jax.ShapeDtypeStruct((count, cells_x, cells_y), F32),
-            jax.ShapeDtypeStruct((count, KW, KW), F32),
+            jax.ShapeDtypeStruct((n_x, piece, 128), F32),
         ),
-        in_specs=[hbm, vmem, vmem, vmem, vmem, vmem, hbm, hbm, vmem, hbm, hbm],
-        out_specs=(vmem, vmem),
+        in_specs=[hbm] * 10,
+        out_specs=(hbm, hbm),
         scratch_shapes=[
+            pltpu.VMEM((count, cells_x, cells_y), F32),
+            pltpu.VMEM(terrain.shape, jnp.int32),
+            pltpu.VMEM(parent_columns.shape, BF16),
+            pltpu.VMEM((1, records), jnp.int32),
+            pltpu.VMEM((record_cells.shape[1], records), jnp.int32),
+            pltpu.VMEM((record_cells.shape[1], records), BF16),
+            pltpu.VMEM(coarse_x.shape, BF16),
             pltpu.VMEM((count, cells_x + 16, cells_y), F32),
             pltpu.VMEM((variables * 64, records), F32),
             pltpu.VMEM((variables * 64, width), F32),
@@ -454,12 +530,10 @@
             pltpu.VMEM((n_y, piece, 128), F32),
             pltpu.VMEM((n_x, piece, 128), F32),
             pltpu.VMEM(project_x.shape[1:], BF16),
-            pltpu.VMEM(expand_x.shape[1:], BF16),
             pltpu.VMEM(along_y.shape[1:], BF16),
             pltpu.VMEM(coarse_y_table.shape[1:], F32),
-            pltpu.VMEM((2, 4 * KW, 4 * cells_y), BF16),
             pltpu.VMEM((lines, 4 * cells_y), F32),
-            dma((5,)),
+            dma((11,)), dma((2 * variables + 1,)),
             dma((n_x,)), dma((n_x,)),
             dma((4,)), dma((4,)),
             dma((n_x,)), dma((n_x,)),
@@ -467,15 +541,34 @@
             dma((n_x,)), dma((n_x,)),
         ],
         compiler_params=pltpu.CompilerParams(
-            collective_id=0, has_side_effects=True, vmem_limit_bytes=48 * 1024 * 1024
+            collective_id=0, has_side_effects=True, vmem_limit_bytes=60 * 1024 * 1024
         ),
         name="nudge",
     )(
         fields.reshape(count, cells_x, cells_y), terrain, parent_columns,
         record_tile.T, record_cells.T, record_weights.T,
-        jnp.asarray(project_x), jnp.asarray(expand_x), jnp.asarray(coarse_x),
-        jnp.asarray(along_y), jnp.asarray(coarse_y_table),
+        jnp.asarray(project_x), jnp.asarray(coarse_x), along_y, jnp.asarray(coarse_y_table),
     )
+    state, coeffs = pl.pallas_call(
+        finish,
+        out_shape=(
+            jax.ShapeDtypeStruct((count, cells_x, cells_y), F32),
+            jax.ShapeDtypeStruct((count, KW, KW), F32),
+        ),
+        in_specs=[hbm] * 4,
+        out_specs=(hbm, hbm),
+        scratch_shapes=[
+            pltpu.VMEM((count, cells_x, cells_y), F32),
+            pltpu.VMEM((n_x, piece, 128), F32),
+            pltpu.VMEM(expand_x.shape[1:], BF16),
+            pltpu.VMEM(along_y.shape[1:], BF16),
+            pltpu.VMEM((count, KW, KW), F32),
+            dma((count // 4 + 3,)),
+            dma((count // 4 + 1,)),
+        ],
+        compiler_params=pltpu.CompilerParams(vmem_limit_bytes=60 * 1024 * 1024),
+        name="finish",
+    )(partial_state, summed, jnp.asarray(expand_x), along_y)
     return state.reshape(fields.shape), coeffs.reshape(variables, levels, KW, KW)
 
 

time: 36.4 us -> 28.9 us (0.79)
  local copies, waits for them, and re-layouts: 11.4 us -> 0 us
  Pallas kernels: 23.8 us -> 28.1 us
    unnamed x24 -> x0, local copies, waits for them, and re-layouts: 11.4 us -> none
    pallas_call x0 -> x1, Pallas kernels: none -> 2.96 us  [per_device(): pl.pallas_call(finish, out_shape=(jax.ShapeDtypeStruct((count, cells_x, c...]
    pallas_call x1, Pallas kernels: 23.8 us -> 25.1 us  [per_device(): pl.pallas_call(functools.partial(body, (n_x, n_y, variables, levels, pare...]
where the time goes in v1:
time: 28.9 us; the launch traced here: 28.7 us
  Pallas kernels  28.1 us (97%)
  between operations  0.64 us (2%)
    pallas_call x1, Pallas kernels, per_device(): pl.pallas_call(functools.partial(body, (n_x, n_y, variables, levels, pare...  25.1 us
    pallas_call x1, Pallas kernels, per_device(): pl.pallas_call(finish, out_shape=(jax.ShapeDtypeStruct((count, cells_x, c...  2.96 us

profile of v1, /device:TPU:0, one launch (start us, length us, event | category | flops | bytes accessed | tf_op | source)
XLA Modules:
  0.0 28.7 jit_solution(3311452489699123930)
XLA Ops:
  0.6 25.1 %nudge.1 = (f32[24,96,128]{2,1,0:T(8,128)}, f32[8,24,128]{2,1,0:T(8,128)}) custom-call(f32[24,96,128]{2,1,0:T(8,128)} %bitcast.6, s32[96,128]{1,0:T(8,128)} %terrain_hbm.1, bf16[3,60,384]{2,1,0:T(8,128)(2,1)} %columns_hbm.1, s32[1,384]{1,0:T(1,128)} %bitcast.9, s32[4,384]{1,0:T(4,128)} %bitcast.7, bf16[4,384]{1,0:T(4,128)(2,1)} %bitcast.8, ...), custom_call_target="tpu_custom_call" | custom-call | tf_op jit(solution)/shard_map/nudge/pallas_call | solution.py:502
  25.8 3.0 %finish.1 = (f32[24,96,128]{2,1,0:T(8,128)}, f32[24,32,32]{2,1,0:T(8,128)}) custom-call(f32[24,96,128]{2,1,0:T(8,128)} %get-tuple-element.6.partial_hbm, f32[8,24,128]{2,1,0:T(8,128)} %get-tuple-element.7.total_hbm, bf16[8,96,96]{2,1,0:T(8,128)(2,1)} %constant.14.clone.expand_x_hbm, bf16[4,2,32,128]{3,2,1,0:T(8,128)(2,1)} %constant.10.clone.along_y_hbm), custom_call_target="tpu_custom_call" | custom-call | tf_op jit(solution)/shard_map/finish/pallas_call | solution.py:552

commit v2 on v1

--- a/solution.py
+++ b/solution.py
@@ -16,7 +16,6 @@
 MESH = pl.DeviceIdType.MESH
 F32 = jnp.float32
 BF16 = jnp.bfloat16
-NT = (((1,), (1,)), ((), ()))
 
 
 def wave_rows(length):
@@ -54,13 +53,16 @@
     high, low = parts(np.transpose(own_x, (0, 2, 1)) * (4.0 * scale))
     expand_x = np.concatenate([high, low, high], 2)
     at_coarse = basis_x[:, ::RATIO] * (RATIO * RATIO * scale)
-    coarse_x = np.kron(np.eye(4), at_coarse)
+    coarse_x = np.transpose(np.kron(np.eye(4), at_coarse))
     coarse_x = np.stack(parts(coarse_x))
     own_y = np.transpose(basis_y.reshape(KW, n_y, cells_y), (1, 0, 2))
     along_y = np.stack(parts(own_y), 1)
+    project_y = np.stack(
+        parts(np.stack([np.kron(np.eye(4), np.transpose(block)) for block in own_y])), 1
+    )
     at_rows = np.transpose(basis_y[:, ::RATIO]).reshape(n_y, coarse_y, KW)
     coarse_y_table = np.stack(parts(np.tile(at_rows, (1, 1, fields_count))), 1).astype(np.float32)
-    return project_x, expand_x, coarse_x, along_y, coarse_y_table
+    return project_x, expand_x, coarse_x, along_y, project_y, coarse_y_table
 
 
 def split(values):
@@ -72,19 +74,15 @@
     return jnp.dot(a, b, preferred_element_type=F32)
 
 
-def dot_nt(a, b):
-    return lax.dot_general(a, b, NT, preferred_element_type=F32)
-
-
 def body(
     sizes,
     fields_hbm, terrain_hbm, columns_hbm, tile_hbm, cells_hbm, weights_hbm,
-    project_x_hbm, coarse_x_hbm, along_y_hbm, coarse_y_hbm,
+    project_x_hbm, coarse_x_hbm, project_y_hbm, coarse_y_hbm,
     state_hbm, total_hbm,
     state, terrain, columns, tile, cells, weights, coarse_x,
     padded, column_rows, coarse, target, heights, heights_got, edge_rows, edge_rows_got,
     edge_columns, edge_columns_got, partial, partial_got, plane, total,
-    project_x, along_y, coarse_y_table, y_terms,
+    project_x, project_y, coarse_y_table, y_terms, ids, amounts,
     load_sem, store_sem, send_h, recv_h, send_e, recv_e, send_r, recv_r, send_p, recv_p, send_t, recv_t,
 ):
     n_x, n_y, variables, levels, parent_levels = sizes
@@ -102,7 +100,7 @@
     loads = [
         pltpu.make_async_copy(fields_hbm, padded.at[:, pl.ds(top, cells_x), :], load_sem.at[0]),
         pltpu.make_async_copy(project_x_hbm.at[me_x], project_x, load_sem.at[1]),
-        pltpu.make_async_copy(along_y_hbm.at[me_y], along_y, load_sem.at[3]),
+        pltpu.make_async_copy(project_y_hbm.at[me_y], project_y, load_sem.at[3]),
         pltpu.make_async_copy(coarse_y_hbm.at[me_y], coarse_y_table, load_sem.at[4]),
         pltpu.make_async_copy(coarse_x_hbm, coarse_x, load_sem.at[5]),
     ]
@@ -155,16 +153,41 @@
     place = cells[...]
     place = (place % tile_y) * row_x + tile[...] * tile_x + place // tile_y
     amount = weights[...].astype(F32)
+    entries = place.shape[0]
+    merged = []
+    for e in range(entries):
+        sum_e = jnp.zeros((1, records), F32)
+        for f in range(entries):
+            sum_e = sum_e + jnp.where(place[f : f + 1] == place[e : e + 1], amount[f : f + 1], 0.0)
+        merged.append(sum_e)
+    listed = jnp.concatenate(
+        [place.astype(F32)] + merged + [jnp.zeros((128 - 2 * entries, records), F32)], axis=0
+    )
+    listed = jnp.transpose(listed)
+    for e in range(entries):
+        named = jnp.broadcast_to(listed[:, e : e + 1], (records, 128))
+        ids[e] = named.astype(jnp.int32).astype(jnp.int16)
+        named = jnp.broadcast_to(listed[:, entries + e : entries + e + 1], (records, 128))
+        amounts[0, e], amounts[1, e] = split(named)
     step = 256 if width % 256 == 0 else 128
+    lane = lax.broadcasted_iota(jnp.int32, (records, 128), 1).astype(jnp.int16)
 
     def spread(i, carry):
-        line = lax.broadcasted_iota(jnp.int32, (step, records), 0) + i * step
-        matrix = jnp.zeros((step, records), F32)
-        for e in range(place.shape[0]):
-            matrix = matrix + jnp.where(place[e : e + 1] == line, amount[e : e + 1], 0.0)
-        high, low = split(matrix)
+        highs, lows = [], []
+        for part in range(step // 128):
+            here = lane + (i * step + part * 128).astype(jnp.int16)
+            high = jnp.zeros((records, 128), BF16)
+            low = jnp.zeros((records, 128), BF16)
+            for e in range(entries):
+                hit = ids[e] == here
+                high = jnp.where(hit, amounts[0, e], high)
+                low = jnp.where(hit, amounts[1, e], low)
+            highs.append(high)
+            lows.append(low)
         at = pl.ds(pl.multiple_of(i * step, step), step)
-        coarse[:, at] = dot_nt(packed, high) + dot_nt(packed, low)
+        coarse[:, at] = dot(packed, jnp.concatenate(highs, axis=1)) + dot(
+            packed, jnp.concatenate(lows, axis=1)
+        )
         return carry
 
     lax.fori_loop(0, width // step, spread, 0)
@@ -187,7 +210,6 @@
     for load in loads:
         load.wait()
 
-    block_y = [diagonal(along_y[part]) for part in range(2)]
     for g in range(count // 4):
         highs, lows = [], []
         for i in range(4 * g, 4 * g + 4):
@@ -200,7 +222,7 @@
         both = dot(project_x[...], stacked)
         y_terms[g * KW : (g + 1) * KW, :] = both[:KW] + both[KW:]
     high, low = split(y_terms[...])
-    nest = dot_nt(high, block_y[0]) + dot_nt(low, block_y[0]) + dot_nt(high, block_y[1])
+    nest = dot(high, project_y[0]) + dot(low, project_y[0]) + dot(high, project_y[1])
 
     lane = lax.broadcasted_iota(jnp.int32, (KW, count * KW), 1)
     row = lax.broadcasted_iota(jnp.int32, (KW, count * KW), 0)
@@ -253,7 +275,8 @@
         lax.fori_loop(0, chunks, interpolate, 0)
 
     high, low = split(target[...])
-    along_x = dot_nt(coarse_x[0], high) + dot_nt(coarse_x[0], low) + dot_nt(coarse_x[1], high)
+    along_x = dot(high, coarse_x[0]) + dot(low, coarse_x[0]) + dot(high, coarse_x[1])
+    along_x = jnp.transpose(along_x)
     along_x = jnp.concatenate([along_x[r * KW : (r + 1) * KW] for r in range(4)], axis=1)
     high, low = split(along_x)
     wanted = dot(high, spread_y[0]) + dot(low, spread_y[0]) + dot(high, spread_y[1])
@@ -493,7 +516,7 @@
     groups = tile_y // 4
     lines = count // 4 * KW
     piece = -(-lines // (8 * n_x)) * 8
-    project_x, expand_x, coarse_x, along_y, coarse_y_table = tables(
+    project_x, expand_x, coarse_x, along_y, project_y, coarse_y_table = tables(
         n_x, n_y, cells_x, cells_y, count
     )
     along_y = jnp.asarray(along_y)
@@ -530,9 +553,11 @@
             pltpu.VMEM((n_y, piece, 128), F32),
             pltpu.VMEM((n_x, piece, 128), F32),
             pltpu.VMEM(project_x.shape[1:], BF16),
-            pltpu.VMEM(along_y.shape[1:], BF16),
+            pltpu.VMEM(project_y.shape[1:], BF16),
             pltpu.VMEM(coarse_y_table.shape[1:], F32),
             pltpu.VMEM((lines, 4 * cells_y), F32),
+            pltpu.VMEM((record_cells.shape[1], records, 128), jnp.int16),
+            pltpu.VMEM((2, record_cells.shape[1], records, 128), BF16),
             dma((11,)), dma((2 * variables + 1,)),
             dma((n_x,)), dma((n_x,)),
             dma((4,)), dma((4,)),
@@ -547,7 +572,7 @@
     )(
         fields.reshape(count, cells_x, cells_y), terrain, parent_columns,
         record_tile.T, record_cells.T, record_weights.T,
-        jnp.asarray(project_x), jnp.asarray(coarse_x), along_y, jnp.asarray(coarse_y_table),
+        jnp.asarray(project_x), jnp.asarray(coarse_x), jnp.asarray(project_y), jnp.asarray(coarse_y_table),
     )
     state, coeffs = pl.pallas_call(
         finish,

time: 28.9 us -> 29.9 us (1.035)
  Pallas kernels: 28.1 us -> 29.1 us
    pallas_call x1, Pallas kernels: 25.1 us -> 26.2 us  [per_device(): pl.pallas_call(functools.partial(body, (n_x, n_y, variables, levels, pare...]
where the time goes in v2:
time: 29.9 us; the launch traced here: 29.8 us
  Pallas kernels  29.1 us (97%)
  between operations  0.64 us (2%)
    pallas_call x1, Pallas kernels, per_device(): pl.pallas_call(functools.partial(body, (n_x, n_y, variables, levels, pare...  26.2 us
    pallas_call x1, Pallas kernels, per_device(): pl.pallas_call(finish, out_shape=(jax.ShapeDtypeStruct((count, cells_x, c...  2.96 us

profile of v2, /device:TPU:0, one launch (start us, length us, event | category | flops | bytes accessed | tf_op | source)
XLA Modules:
  0.0 29.8 jit_solution(6545834530532789015)
XLA Ops:
  0.6 26.2 %nudge.1 = (f32[24,96,128]{2,1,0:T(8,128)}, f32[8,24,128]{2,1,0:T(8,128)}) custom-call(f32[24,96,128]{2,1,0:T(8,128)} %bitcast.6, s32[96,128]{1,0:T(8,128)} %terrain_hbm.1, bf16[3,60,384]{2,1,0:T(8,128)(2,1)} %columns_hbm.1, s32[1,384]{1,0:T(1,128)} %bitcast.9, s32[4,384]{1,0:T(4,128)} %bitcast.7, bf16[4,384]{1,0:T(4,128)(2,1)} %bitcast.8, ...), custom_call_target="tpu_custom_call" | custom-call | tf_op jit(solution)/shard_map/nudge/pallas_call | solution.py:525
  26.8 3.0 %finish.1 = (f32[24,96,128]{2,1,0:T(8,128)}, f32[24,32,32]{2,1,0:T(8,128)}) custom-call(f32[24,96,128]{2,1,0:T(8,128)} %get-tuple-element.6.partial_hbm, f32[8,24,128]{2,1,0:T(8,128)} %get-tuple-element.7.total_hbm, bf16[8,96,96]{2,1,0:T(8,128)(2,1)} %constant.17.clone.expand_x_hbm, bf16[4,2,32,128]{3,2,1,0:T(8,128)(2,1)} %constant.12.clone.along_y_hbm), custom_call_target="tpu_custom_call" | custom-call | tf_op jit(solution)/shard_map/finish/pallas_call | solution.py:577

commit v3 on v1

--- a/solution.py
+++ b/solution.py
@@ -155,16 +155,30 @@
     place = cells[...]
     place = (place % tile_y) * row_x + tile[...] * tile_x + place // tile_y
     amount = weights[...].astype(F32)
+    entries = place.shape[0]
+    merged = []
+    for e in range(entries):
+        sum_e = jnp.zeros((1, records), F32)
+        for f in range(entries):
+            sum_e = sum_e + jnp.where(place[f : f + 1] == place[e : e + 1], amount[f : f + 1], 0.0)
+        merged.append(sum_e)
     step = 256 if width % 256 == 0 else 128
+    line = lax.broadcasted_iota(jnp.int32, (32, records), 0)
 
     def spread(i, carry):
-        line = lax.broadcasted_iota(jnp.int32, (step, records), 0) + i * step
-        matrix = jnp.zeros((step, records), F32)
-        for e in range(place.shape[0]):
-            matrix = matrix + jnp.where(place[e : e + 1] == line, amount[e : e + 1], 0.0)
-        high, low = split(matrix)
+        highs, lows = [], []
+        for part in range(step // 32):
+            here = place - (i * step + part * 32)
+            matrix = jnp.zeros((32, records), F32)
+            for e in range(entries):
+                matrix = jnp.where(here[e : e + 1] == line, merged[e], matrix)
+            high, low = split(matrix)
+            highs.append(high)
+            lows.append(low)
         at = pl.ds(pl.multiple_of(i * step, step), step)
-        coarse[:, at] = dot_nt(packed, high) + dot_nt(packed, low)
+        coarse[:, at] = dot_nt(packed, jnp.concatenate(highs, axis=0)) + dot_nt(
+            packed, jnp.concatenate(lows, axis=0)
+        )
         return carry
 
     lax.fori_loop(0, width // step, spread, 0)
@@ -200,7 +214,8 @@
         both = dot(project_x[...], stacked)
         y_terms[g * KW : (g + 1) * KW, :] = both[:KW] + both[KW:]
     high, low = split(y_terms[...])
-    nest = dot_nt(high, block_y[0]) + dot_nt(low, block_y[0]) + dot_nt(high, block_y[1])
+    nest = dot_nt(jnp.concatenate([high, low], axis=0), block_y[0])
+    nest = nest[: high.shape[0]] + nest[high.shape[0] :] + dot_nt(high, block_y[1])
 
     lane = lax.broadcasted_iota(jnp.int32, (KW, count * KW), 1)
     row = lax.broadcasted_iota(jnp.int32, (KW, count * KW), 0)
@@ -256,7 +271,8 @@
     along_x = dot_nt(coarse_x[0], high) + dot_nt(coarse_x[0], low) + dot_nt(coarse_x[1], high)
     along_x = jnp.concatenate([along_x[r * KW : (r + 1) * KW] for r in range(4)], axis=1)
     high, low = split(along_x)
-    wanted = dot(high, spread_y[0]) + dot(low, spread_y[0]) + dot(high, spread_y[1])
+    wanted = dot(jnp.concatenate([high, low], axis=0), spread_y[0])
+    wanted = wanted[:KW] + wanted[KW:] + dot(high, spread_y[1])
 
     lines = count // 4 * KW
     difference = [
@@ -323,36 +339,39 @@
     for copy, out, _ in edges:
         pl.when(out)(copy.start)
 
-    metric = TOP / (TOP - terrain[...].astype(F32))
-    metric = 0.1 * (metric * metric)
+    rows = 32
 
     def advance(k, carry):
-        wind_x = 0.05 * padded[k, top : top + cells_x, :]
-        wind_y = 0.05 * padded[levels + k, top : top + cells_x, :]
         above_k = jnp.minimum(k + 1, levels - 1)
         below_k = jnp.maximum(k - 1, 0)
-        lane = lax.broadcasted_iota(jnp.int32, (cells_x, cells_y), 1)
-        for v in range(variables):
-            i = v * levels + k
-            q = padded[i, top : top + cells_x, :]
-            east = padded[i, top + 1 : top + 1 + cells_x, :]
-            west = padded[i, top - 1 : top - 1 + cells_x, :]
-            north = jnp.where(
-                lane == cells_y - 1,
-                pltpu.roll(edge_columns_got[0], cells_y - 1 - i, 1),
-                pltpu.roll(q, cells_y - 1, 1),
-            )
-            south = jnp.where(
-                lane == 0,
-                pltpu.roll(edge_columns_got[1], lax.rem(cells_y - i, cells_y), 1),
-                pltpu.roll(q, 1, 1),
-            )
-            above = padded[v * levels + above_k, top : top + cells_x, :]
-            below = padded[v * levels + below_k, top : top + cells_x, :]
-            transport = wind_x * (east - west) + wind_y * (north - south)
-            diffusion = 0.1 * ((east + west) + (north + south) - 4.0 * q)
-            mixing = metric * ((above + below) - 2.0 * q)
-            state[i] = q - transport + diffusion + mixing
+        lane = lax.broadcasted_iota(jnp.int32, (rows, cells_y), 1)
+        for r in range(0, cells_x, rows):
+            here = slice(top + r, top + r + rows)
+            metric = TOP / (TOP - terrain[r : r + rows].astype(F32))
+            metric = 0.1 * (metric * metric)
+            wind_x = 0.05 * padded[k, here, :]
+            wind_y = 0.05 * padded[levels + k, here, :]
+            for v in range(variables):
+                i = v * levels + k
+                q = padded[i, here, :]
+                east = padded[i, top + r + 1 : top + r + 1 + rows, :]
+                west = padded[i, top + r - 1 : top + r - 1 + rows, :]
+                north = jnp.where(
+                    lane == cells_y - 1,
+                    pltpu.roll(edge_columns_got[0, r : r + rows], cells_y - 1 - i, 1),
+                    pltpu.roll(q, cells_y - 1, 1),
+                )
+                south = jnp.where(
+                    lane == 0,
+                    pltpu.roll(edge_columns_got[1, r : r + rows], lax.rem(cells_y - i, cells_y), 1),
+                    pltpu.roll(q, 1, 1),
+                )
+                above = padded[v * levels + above_k, here, :]
+                below = padded[v * levels + below_k, here, :]
+                transport = wind_x * (east - west) + wind_y * (north - south)
+                diffusion = 0.1 * ((east + west) + (north + south) - 4.0 * q)
+                mixing = metric * ((above + below) - 2.0 * q)
+                state[i, r : r + rows] = q - transport + diffusion + mixing
         return carry
 
     half_levels = levels // 2
@@ -465,7 +484,8 @@
     stores[0].start()
     high, low = split(summed)
     block = diagonal(along_y[0])
-    along = dot(high, block) + dot(low, block) + dot(high, diagonal(along_y[1]))
+    along = dot(jnp.concatenate([high, low], axis=0), block)
+    along = along[:lines] + along[lines:] + dot(high, diagonal(along_y[1]))
     for g in range(count // 4):
         high, low = split(along[g * KW : (g + 1) * KW])
         modes = dot(expand_x[...], jnp.concatenate([high, high, low], axis=0))

time: 28.9 us -> 28.9 us (level)
  no operation moved by 1% of the time
where the time goes in v3:
time: 28.9 us; the launch traced here: 28.7 us
  Pallas kernels  28.1 us (97%)
  between operations  0.64 us (2%)
    pallas_call x1, Pallas kernels, per_device(): pl.pallas_call(functools.partial(body, (n_x, n_y, variables, levels, pare...  25.1 us
    pallas_call x1, Pallas kernels, per_device(): pl.pallas_call(finish, out_shape=(jax.ShapeDtypeStruct((count, cells_x, c...  2.96 us

profile of v3, /device:TPU:0, one launch (start us, length us, event | category | flops | bytes accessed | tf_op | source)
XLA Modules:
  0.0 28.7 jit_solution(15891963981494802812)
XLA Ops:
  0.6 25.1 %nudge.1 = (f32[24,96,128]{2,1,0:T(8,128)}, f32[8,24,128]{2,1,0:T(8,128)}) custom-call(f32[24,96,128]{2,1,0:T(8,128)} %bitcast.6, s32[96,128]{1,0:T(8,128)} %terrain_hbm.1, bf16[3,60,384]{2,1,0:T(8,128)(2,1)} %columns_hbm.1, s32[1,384]{1,0:T(1,128)} %bitcast.9, s32[4,384]{1,0:T(4,128)} %bitcast.7, bf16[4,384]{1,0:T(4,128)(2,1)} %bitcast.8, ...), custom_call_target="tpu_custom_call" | custom-call | tf_op jit(solution)/shard_map/nudge/pallas_call | solution.py:522
  25.7 3.0 %finish.1 = (f32[24,96,128]{2,1,0:T(8,128)}, f32[24,32,32]{2,1,0:T(8,128)}) custom-call(f32[24,96,128]{2,1,0:T(8,128)} %get-tuple-element.6.partial_hbm, f32[8,24,128]{2,1,0:T(8,128)} %get-tuple-element.7.total_hbm, bf16[8,96,96]{2,1,0:T(8,128)(2,1)} %constant.14.clone.expand_x_hbm, bf16[4,2,32,128]{3,2,1,0:T(8,128)(2,1)} %constant.10.clone.along_y_hbm), custom_call_target="tpu_custom_call" | custom-call | tf_op jit(solution)/shard_map/finish/pallas_call | solution.py:572

commit v4 on v3

--- a/solution.py
+++ b/solution.py
@@ -83,7 +83,7 @@
     state_hbm, total_hbm,
     state, terrain, columns, tile, cells, weights, coarse_x,
     padded, column_rows, coarse, target, heights, heights_got, edge_rows, edge_rows_got,
-    edge_columns, edge_columns_got, partial, partial_got, plane, total,
+    edge_columns, edge_columns_got, turned, partial, partial_got, plane, total,
     project_x, along_y, coarse_y_table, y_terms,
     load_sem, store_sem, send_h, recv_h, send_e, recv_e, send_r, recv_r, send_p, recv_p, send_t, recv_t,
 ):
@@ -146,6 +146,21 @@
         here = jnp.where(lane % row_x - me_x * tile_x == row, here, 0.0)
         heights[g : g + 1, :] = jnp.sum(here, axis=0, keepdims=True)
 
+    pl.semaphore_wait(barrier, n_x + n_y - 2)
+    sends_h = []
+    for d in range(1, n_x):
+        sends_h.append(
+            pltpu.make_async_remote_copy(
+                src_ref=heights,
+                dst_ref=heights_got.at[d],
+                send_sem=send_h.at[d],
+                recv_sem=recv_h.at[d],
+                device_id=(lax.rem(me_x + d, n_x), me_y),
+                device_id_type=MESH,
+            )
+        )
+        sends_h[-1].start()
+
     for load in early[1:]:
         load.wait()
     column_rows[...] = jnp.zeros_like(column_rows)
@@ -182,21 +197,6 @@
         return carry
 
     lax.fori_loop(0, width // step, spread, 0)
-
-    pl.semaphore_wait(barrier, n_x + n_y - 2)
-    sends_h = []
-    for d in range(1, n_x):
-        sends_h.append(
-            pltpu.make_async_remote_copy(
-                src_ref=heights,
-                dst_ref=heights_got.at[d],
-                send_sem=send_h.at[d],
-                recv_sem=recv_h.at[d],
-                device_id=(lax.rem(me_x + d, n_x), me_y),
-                device_id_type=MESH,
-            )
-        )
-        sends_h[-1].start()
 
     for load in loads:
         load.wait()
@@ -311,8 +311,11 @@
         q = padded[i, top : top + cells_x, :]
         first = jnp.where(lane == i, q if i == 0 else pltpu.roll(q, i, 1), first)
         last = jnp.where(lane == i, pltpu.roll(q, i + 1, 1), last)
-    edge_columns[0] = first
-    edge_columns[1] = last
+    for side, columns_here in enumerate((first, last)):
+        columns_here = jnp.concatenate(
+            [columns_here, jnp.zeros((cells_y - cells_x, cells_y), F32)], axis=0
+        )
+        edge_columns[side] = jnp.transpose(columns_here)[:count]
 
     def edge_copy(source, got, side, slot, device):
         return pltpu.make_async_remote_copy(
@@ -358,12 +361,12 @@
                 west = padded[i, top + r - 1 : top + r - 1 + rows, :]
                 north = jnp.where(
                     lane == cells_y - 1,
-                    pltpu.roll(edge_columns_got[0, r : r + rows], cells_y - 1 - i, 1),
+                    pltpu.roll(turned[0, r : r + rows], cells_y - 1 - i, 1),
                     pltpu.roll(q, cells_y - 1, 1),
                 )
                 south = jnp.where(
                     lane == 0,
-                    pltpu.roll(edge_columns_got[1, r : r + rows], lax.rem(cells_y - i, cells_y), 1),
+                    pltpu.roll(turned[1, r : r + rows], lax.rem(cells_y - i, cells_y), 1),
                     pltpu.roll(q, 1, 1),
                 )
                 above = padded[v * levels + above_k, here, :]
@@ -397,6 +400,11 @@
     for copy, out, arrives in edges:
         pl.when(out)(copy.wait_send)
         pl.when(arrives)(copy.wait_recv)
+    for side in range(2):
+        columns_here = jnp.concatenate(
+            [edge_columns_got[side], jnp.zeros((cells_y - count, cells_y), F32)], axis=0
+        )
+        turned[side] = jnp.transpose(columns_here)[:cells_x]
     padded[:, top + cells_x, :] = edge_rows_got[0]
     padded[:, top - 1, :] = edge_rows_got[1]
 
@@ -543,7 +551,8 @@
             pltpu.VMEM((n_x, groups, 4 * row_x), F32),
             pltpu.VMEM((2, count, cells_y), F32),
             pltpu.VMEM((2, count, cells_y), F32),
-            pltpu.VMEM((2, cells_x, cells_y), F32),
+            pltpu.VMEM((2, count, cells_y), F32),
+            pltpu.VMEM((2, count, cells_y), F32),
             pltpu.VMEM((2, cells_x, cells_y), F32),
             pltpu.VMEM((n_x, piece, 128), F32),
             pltpu.VMEM((n_x, piece, 128), F32),

time: 28.9 us -> 27 us (0.934)
  Pallas kernels: 28.1 us -> 26.2 us
    pallas_call x1, Pallas kernels: 25.1 us -> 23.3 us  [per_device(): pl.pallas_call(functools.partial(body, (n_x, n_y, variables, levels, pare...]
where the time goes in v4:
time: 27 us; the launch traced here: 26.9 us
  Pallas kernels  26.2 us (97%)
  between operations  0.64 us (2%)
    pallas_call x1, Pallas kernels, per_device(): pl.pallas_call(functools.partial(body, (n_x, n_y, variables, levels, pare...  23.3 us
    pallas_call x1, Pallas kernels, per_device(): pl.pallas_call(finish, out_shape=(jax.ShapeDtypeStruct((count, cells_x, c...  2.96 us

profile of v4, /device:TPU:0, one launch (start us, length us, event | category | flops | bytes accessed | tf_op | source)
XLA Modules:
  0.0 26.9 jit_solution(6593643985689925690)
XLA Ops:
  0.6 23.3 %nudge.1 = (f32[24,96,128]{2,1,0:T(8,128)}, f32[8,24,128]{2,1,0:T(8,128)}) custom-call(f32[24,96,128]{2,1,0:T(8,128)} %bitcast.6, s32[96,128]{1,0:T(8,128)} %terrain_hbm.1, bf16[3,60,384]{2,1,0:T(8,128)(2,1)} %columns_hbm.1, s32[1,384]{1,0:T(1,128)} %bitcast.9, s32[4,384]{1,0:T(4,128)} %bitcast.7, bf16[4,384]{1,0:T(4,128)(2,1)} %bitcast.8, ...), custom_call_target="tpu_custom_call" | custom-call | tf_op jit(solution)/shard_map/nudge/pallas_call | solution.py:530
  23.9 3.0 %finish.1 = (f32[24,96,128]{2,1,0:T(8,128)}, f32[24,32,32]{2,1,0:T(8,128)}) custom-call(f32[24,96,128]{2,1,0:T(8,128)} %get-tuple-element.6.partial_hbm, f32[8,24,128]{2,1,0:T(8,128)} %get-tuple-element.7.total_hbm, bf16[8,96,96]{2,1,0:T(8,128)(2,1)} %constant.14.clone.expand_x_hbm, bf16[4,2,32,128]{3,2,1,0:T(8,128)(2,1)} %constant.10.clone.along_y_hbm), custom_call_target="tpu_custom_call" | custom-call | tf_op jit(solution)/shard_map/finish/pallas_call | solution.py:581

commit v5 on v4

--- a/solution.py
+++ b/solution.py
@@ -287,20 +287,24 @@
         )
     for i in range(n_x):
         partial[i] = difference[i * piece : (i + 1) * piece]
+    cuts = [0, piece // 16 * 8, piece] if piece > 8 else [0, piece]
+    slabs = [pl.ds(a, b - a) for a, b in zip(cuts[:-1], cuts[1:])]
     sends_r = []
-    for d in range(1, n_x):
-        to = lax.rem(me_x + d, n_x)
-        sends_r.append(
-            pltpu.make_async_remote_copy(
-                src_ref=partial.at[to],
-                dst_ref=partial_got.at[d],
-                send_sem=send_r.at[d],
-                recv_sem=recv_r.at[d],
-                device_id=(to, me_y),
-                device_id_type=MESH,
+    for part, slab in enumerate(slabs):
+        sends_r.append([])
+        for d in range(1, n_x):
+            to = lax.rem(me_x + d, n_x)
+            sends_r[part].append(
+                pltpu.make_async_remote_copy(
+                    src_ref=partial.at[to, slab],
+                    dst_ref=partial_got.at[d, slab],
+                    send_sem=send_r.at[part, d],
+                    recv_sem=recv_r.at[part, d],
+                    device_id=(to, me_y),
+                    device_id_type=MESH,
+                )
             )
-        )
-        sends_r[-1].start()
+            sends_r[part][-1].start()
 
     edge_rows[0] = padded[:, top, :]
     edge_rows[1] = padded[:, top + cells_x - 1, :]
@@ -378,25 +382,27 @@
         return carry
 
     half_levels = levels // 2
-    for copy in sends_r:
-        copy.wait()
-    mine = partial[me_x]
-    for d in range(1, n_x):
-        mine = mine + partial_got[d]
-    plane[me_y] = mine
     sends_p = []
-    for d in range(1, n_y):
-        sends_p.append(
-            pltpu.make_async_remote_copy(
-                src_ref=plane.at[me_y],
-                dst_ref=plane.at[me_y],
-                send_sem=send_p.at[d],
-                recv_sem=recv_p.at[d],
-                device_id=(me_x, lax.rem(me_y + d, n_y)),
-                device_id_type=MESH,
+    for part, slab in enumerate(slabs):
+        for copy in sends_r[part]:
+            copy.wait()
+        mine = partial[me_x, slab]
+        for d in range(1, n_x):
+            mine = mine + partial_got[d, slab]
+        plane[me_y, slab] = mine
+        sends_p.append([])
+        for d in range(1, n_y):
+            sends_p[part].append(
+                pltpu.make_async_remote_copy(
+                    src_ref=plane.at[me_y, slab],
+                    dst_ref=plane.at[me_y, slab],
+                    send_sem=send_p.at[part, d],
+                    recv_sem=recv_p.at[part, d],
+                    device_id=(me_x, lax.rem(me_y + d, n_y)),
+                    device_id_type=MESH,
+                )
             )
-        )
-        sends_p[-1].start()
+            sends_p[part][-1].start()
     for copy, out, arrives in edges:
         pl.when(out)(copy.wait_send)
         pl.when(arrives)(copy.wait_recv)
@@ -420,25 +426,26 @@
             )
     for store in stores[:variables]:
         store.start()
-    for copy in sends_p:
-        copy.wait()
-    mine = plane[0]
-    for j in range(1, n_y):
-        mine = mine + plane[j]
-    total[me_x] = mine
     sends_t = []
-    for d in range(1, n_x):
-        sends_t.append(
-            pltpu.make_async_remote_copy(
-                src_ref=total.at[me_x],
-                dst_ref=total.at[me_x],
-                send_sem=send_t.at[d],
-                recv_sem=recv_t.at[d],
-                device_id=(lax.rem(me_x + d, n_x), me_y),
-                device_id_type=MESH,
+    for part, slab in enumerate(slabs):
+        for copy in sends_p[part]:
+            copy.wait()
+        mine = plane[0, slab]
+        for j in range(1, n_y):
+            mine = mine + plane[j, slab]
+        total[me_x, slab] = mine
+        for d in range(1, n_x):
+            sends_t.append(
+                pltpu.make_async_remote_copy(
+                    src_ref=total.at[me_x, slab],
+                    dst_ref=total.at[me_x, slab],
+                    send_sem=send_t.at[part, d],
+                    recv_sem=recv_t.at[part, d],
+                    device_id=(lax.rem(me_x + d, n_x), me_y),
+                    device_id_type=MESH,
+                )
             )
-        )
-        sends_t[-1].start()
+            sends_t[-1].start()
     lax.fori_loop(half_levels, levels, advance, 0)
     for store in stores[variables:]:
         store.start()
@@ -565,9 +572,9 @@
             dma((11,)), dma((2 * variables + 1,)),
             dma((n_x,)), dma((n_x,)),
             dma((4,)), dma((4,)),
-            dma((n_x,)), dma((n_x,)),
-            dma((n_y,)), dma((n_y,)),
-            dma((n_x,)), dma((n_x,)),
+            dma((2, n_x)), dma((2, n_x)),
+            dma((2, n_y)), dma((2, n_y)),
+            dma((2, n_x)), dma((2, n_x)),
         ],
         compiler_params=pltpu.CompilerParams(
             collective_id=0, has_side_effects=True, vmem_limit_bytes=60 * 1024 * 1024

time: 27 us -> 27.3 us (1.011)
  Pallas kernels: 26.2 us -> 26.5 us
    pallas_call x1, Pallas kernels: 23.3 us -> 23.6 us  [per_device(): pl.pallas_call(functools.partial(body, (n_x, n_y, variables, levels, pare...]
where the time goes in v5:
time: 27.3 us; the launch traced here: 27.2 us
  Pallas kernels  26.5 us (97%)
  between operations  0.64 us (2%)
    pallas_call x1, Pallas kernels, per_device(): pl.pallas_call(functools.partial(body, (n_x, n_y, variables, levels, pare...  23.6 us
    pallas_call x1, Pallas kernels, per_device(): pl.pallas_call(finish, out_shape=(jax.ShapeDtypeStruct((count, cells_x, c...  2.96 us

profile of v5, /device:TPU:0, one launch (start us, length us, event | category | flops | bytes accessed | tf_op | source)
XLA Modules:
  0.0 27.2 jit_solution(13924151310076665154)
XLA Ops:
  0.6 23.6 %nudge.1 = (f32[24,96,128]{2,1,0:T(8,128)}, f32[8,24,128]{2,1,0:T(8,128)}) custom-call(f32[24,96,128]{2,1,0:T(8,128)} %bitcast.6, s32[96,128]{1,0:T(8,128)} %terrain_hbm.1, bf16[3,60,384]{2,1,0:T(8,128)(2,1)} %columns_hbm.1, s32[1,384]{1,0:T(1,128)} %bitcast.9, s32[4,384]{1,0:T(4,128)} %bitcast.7, bf16[4,384]{1,0:T(4,128)(2,1)} %bitcast.8, ...), custom_call_target="tpu_custom_call" | custom-call | tf_op jit(solution)/shard_map/nudge/pallas_call | solution.py:537
  24.2 3.0 %finish.1 = (f32[24,96,128]{2,1,0:T(8,128)}, f32[24,32,32]{2,1,0:T(8,128)}) custom-call(f32[24,96,128]{2,1,0:T(8,128)} %get-tuple-element.6.partial_hbm, f32[8,24,128]{2,1,0:T(8,128)} %get-tuple-element.7.total_hbm, bf16[8,96,96]{2,1,0:T(8,128)(2,1)} %constant.14.clone.expand_x_hbm, bf16[4,2,32,128]{3,2,1,0:T(8,128)(2,1)} %constant.10.clone.along_y_hbm), custom_call_target="tpu_custom_call" | custom-call | tf_op jit(solution)/shard_map/finish/pallas_call | solution.py:588

commit v6 on v4

--- a/solution.py
+++ b/solution.py
@@ -78,10 +78,10 @@
 
 def body(
     sizes,
-    fields_hbm, terrain_hbm, columns_hbm, tile_hbm, cells_hbm, weights_hbm,
+    fields_hbm, terrain_hbm, columns, tile_hbm, cells_hbm, weights,
     project_x_hbm, coarse_x_hbm, along_y_hbm, coarse_y_hbm,
     state_hbm, total_hbm,
-    state, terrain, columns, tile, cells, weights, coarse_x,
+    state, terrain, tile, cells, coarse_x,
     padded, column_rows, coarse, target, heights, heights_got, edge_rows, edge_rows_got,
     edge_columns, edge_columns_got, turned, partial, partial_got, plane, total,
     project_x, along_y, coarse_y_table, y_terms,
@@ -108,10 +108,8 @@
     ]
     early = [
         pltpu.make_async_copy(terrain_hbm, terrain, load_sem.at[6]),
-        pltpu.make_async_copy(columns_hbm, columns, load_sem.at[7]),
         pltpu.make_async_copy(tile_hbm, tile, load_sem.at[8]),
         pltpu.make_async_copy(cells_hbm, cells, load_sem.at[9]),
-        pltpu.make_async_copy(weights_hbm, weights, load_sem.at[10]),
     ]
     for load in early:
         load.start()
@@ -525,6 +523,7 @@
         n_x, n_y, cells_x, cells_y, count
     )
     along_y = jnp.asarray(along_y)
+    vmem = pl.BlockSpec(memory_space=pltpu.VMEM)
     hbm = pl.BlockSpec(memory_space=pltpu.HBM)
     dma = pltpu.SemaphoreType.DMA
     partial_state, summed = pl.pallas_call(
@@ -533,15 +532,13 @@
             jax.ShapeDtypeStruct((count, cells_x, cells_y), F32),
             jax.ShapeDtypeStruct((n_x, piece, 128), F32),
         ),
-        in_specs=[hbm] * 10,
+        in_specs=[hbm, hbm, vmem, hbm, hbm, vmem] + [hbm] * 4,
         out_specs=(hbm, hbm),
         scratch_shapes=[
             pltpu.VMEM((count, cells_x, cells_y), F32),
             pltpu.VMEM(terrain.shape, jnp.int32),
-            pltpu.VMEM(parent_columns.shape, BF16),
             pltpu.VMEM((1, records), jnp.int32),
             pltpu.VMEM((record_cells.shape[1], records), jnp.int32),
-            pltpu.VMEM((record_cells.shape[1], records), BF16),
             pltpu.VMEM(coarse_x.shape, BF16),
             pltpu.VMEM((count, cells_x + 16, cells_y), F32),
             pltpu.VMEM((variables * 64, records), F32),

time: 27 us -> 27.9 us (1.033)
  Pallas kernels: 26.2 us -> 27.1 us
    pallas_call x1, Pallas kernels: 23.3 us -> 24.1 us  [per_device(): pl.pallas_call(functools.partial(body, (n_x, n_y, variables, levels, pare...]
where the time goes in v6:
time: 27.9 us; the launch traced here: 27.7 us
  Pallas kernels  27.1 us (97%)
  between operations  0.64 us (2%)
    pallas_call x1, Pallas kernels, per_device(): pl.pallas_call(functools.partial(body, (n_x, n_y, variables, levels, pare...  24.1 us
    pallas_call x1, Pallas kernels, per_device(): pl.pallas_call(finish, out_shape=(jax.ShapeDtypeStruct((count, cells_x, c...  2.96 us

profile of v6, /device:TPU:0, one launch (start us, length us, event | category | flops | bytes accessed | tf_op | source)
XLA Modules:
  0.0 27.7 jit_solution(8783026016051907273)
XLA Ops:
  0.6 24.1 %nudge.1 = (f32[24,96,128]{2,1,0:T(8,128)}, f32[8,24,128]{2,1,0:T(8,128)}) custom-call(f32[24,96,128]{2,1,0:T(8,128)} %bitcast.6, s32[96,128]{1,0:T(8,128)} %terrain_hbm.1, bf16[3,60,384]{2,1,0:T(8,128)(2,1)} %columns.1, s32[1,384]{1,0:T(1,128)} %bitcast.9, s32[4,384]{1,0:T(4,128)} %bitcast.7, bf16[4,384]{1,0:T(4,128)(2,1)} %bitcast.8, ...), custom_call_target="tpu_custom_call" | custom-call | tf_op jit(solution)/shard_map/nudge/pallas_call | solution.py:529
  24.8 3.0 %finish.1 = (f32[24,96,128]{2,1,0:T(8,128)}, f32[24,32,32]{2,1,0:T(8,128)}) custom-call(f32[24,96,128]{2,1,0:T(8,128)} %get-tuple-element.6.partial_hbm, f32[8,24,128]{2,1,0:T(8,128)} %get-tuple-element.7.total_hbm, bf16[8,96,96]{2,1,0:T(8,128)(2,1)} %constant.14.clone.expand_x_hbm, bf16[4,2,32,128]{3,2,1,0:T(8,128)(2,1)} %constant.10.clone.along_y_hbm), custom_call_target="tpu_custom_call" | custom-call | tf_op jit(solution)/shard_map/finish/pallas_call | solution.py:578
